TPU v7x, 128 devices: a whole 4x4x4 slice. The times are simulated.
128 devices in a mesh: energy: 16 (over x_lo, y, core), layer: 8 (over z, x_hi).
Axes of the slice: x: 4 (x_hi: 2, x_lo: 2; x = x_hi * 2 + x_lo), y: 4, z: 4, core: 2. Of those that a mesh axis runs over, the one named last changes fastest.
Arguments:
- green: bfloat16 [512, 8, 256, 256], P('energy', 'layer'), may hold values from -6 to 6
- gradient: bfloat16 [8, 256, 256], P('layer'), may hold values from -0.375 to 0.375
- left_coupling: bfloat16 [8, 256, 128], P('layer'), may hold values from -0.5 to 0.5
- right_coupling: bfloat16 [8, 256, 128], P('layer'), may hold values from -0.5 to 0.5
- dynamical: float32 [8, 256, 256], P('layer'), may hold values from -0.2 to 3
- omega_sq: float32 [16], replicated, may hold values from 1 to 4
- shifts: int32 [16], replicated, may hold values from 1 to 32, as said below
Outputs:
- phonon_self: float32 [16, 8, 256, 256], P('energy', 'layer')
- phonon_green: float32 [16, 8, 256, 256], P('energy', 'layer')
- electron_self: bfloat16 [512, 8, 256, 256], P('energy', 'layer')
Inputs may be any that keep to these rules, and one draw needn't show every extreme that they name: `shifts`: the largest shift is 32.
All inputs are finite; a program needn't handle non-finite values.
Results may differ from a plain program's by a relative error of at most 0.017.
Values may be sent and summed in bfloat16 or wider, within the bound.
A program may use at most 192 MiB of HBM per device.

v0:
```python
import math

import jax
import jax.numpy as jnp
from jax import lax
from jax.sharding import PartitionSpec as P

NEWTON = 3


coupling = 0.01


def shifted(value, axis, steps):
    count = lax.axis_size(axis)
    leading, last = (max(0, -steps), min(count, count - steps))
    return lax.ppermute(value, axis, [(source, source + steps) for source in range(leading, last)])


def in_blocks(x, dim, count):
    dims = x.shape
    tiles = x.reshape(*dims[:dim], count, dims[dim] // count, *dims[dim + 1 :])
    return jnp.moveaxis(tiles, dim, 0)


def sent_and_summed(x, axis, dim):
    tiles = in_blocks(x, dim, lax.axis_size(axis))
    arrived = lax.all_to_all(tiles, axis, split_axis=0, concat_axis=0, tiled=True)
    return arrived.astype(jnp.float32).sum(axis=0)


def joined_along(tiles, dim):
    tiles = jnp.moveaxis(tiles, 0, dim)
    dims = tiles.shape
    return tiles.reshape(*dims[:dim], dims[dim] * dims[dim + 1], *dims[dim + 2 :])


def copy_for_each(x, axis):
    copies = jnp.broadcast_to(x, (lax.axis_size(axis), *x.shape))
    return lax.all_to_all(copies, axis, split_axis=0, concat_axis=0, tiled=True)


def gather_directly(x, axis, dim):
    return joined_along(copy_for_each(x, axis), dim)


def invert(matrix):
    identity = jnp.eye(matrix.shape[-1], dtype=jnp.float32)
    diagonal = jnp.diagonal(matrix, axis1=1, axis2=2)
    approx = identity[None] / diagonal[:, None, :]
    for repeat in range(NEWTON):
        product = jnp.einsum("kij,kjl->kil", matrix, approx, precision=lax.Precision.HIGHEST)
        approx = 2.0 * approx - jnp.einsum(
            "kij,kjl->kil", approx, product, precision=lax.Precision.HIGHEST
        )
    return approx


def body(green, gradient, left_coupling, right_coupling, dynamical, omega_sq, shifts):
    blocks = green[:, 0]
    layer_grad = gradient[0]
    left_cpl = left_coupling[0]
    right_cpl = right_coupling[0]
    stiffness = dynamical[0]
    per_device = blocks.shape[0]
    order = blocks.shape[-1]
    surface = left_cpl.shape[-1]
    frequencies = shifts.shape[0]
    groups = lax.axis_size("energy")
    owned_count = frequencies // groups
    scale = 1.0 / math.sqrt(per_device * groups)
    left_in = shifted(blocks[:, order - surface :, order - surface :], "layer", 1)
    right_in = shifted(blocks[:, :surface, :surface], "layer", -1)
    first_half = jnp.einsum(
        "ij,ejk->eik", layer_grad, blocks, preferred_element_type=jnp.float32
    ).astype(jnp.bfloat16)
    summed = jnp.einsum("eij,kj->eik", first_half, layer_grad, preferred_element_type=jnp.float32)
    left_part = jnp.einsum(
        "ij,ejk->eik", left_cpl, left_in, preferred_element_type=jnp.float32
    ).astype(jnp.bfloat16)
    summed = summed + jnp.einsum(
        "eij,kj->eik", left_part, left_cpl, preferred_element_type=jnp.float32
    )
    right_part = jnp.einsum(
        "ij,ejk->eik", right_cpl, right_in, preferred_element_type=jnp.float32
    ).astype(jnp.bfloat16)
    summed = summed + jnp.einsum(
        "eij,kj->eik", right_part, right_cpl, preferred_element_type=jnp.float32
    )
    sandwich = summed.astype(jnp.bfloat16)
    lower_in = shifted(sandwich, "energy", 1)
    sandwich_window = jnp.concatenate([lower_in, sandwich], axis=0)

    def phonon_term(offset):
        window_part = lax.dynamic_slice_in_dim(sandwich_window, per_device - offset, per_device, 0)
        return jnp.einsum("ern,ern->rn", window_part, blocks, preferred_element_type=jnp.float32)

    partial_self = lax.map(phonon_term, shifts) * scale
    identity = jnp.eye(order, dtype=jnp.float32)
    start_owned = lax.axis_index("energy") * owned_count
    owned_self = sent_and_summed(partial_self.astype(jnp.bfloat16), "energy", 0)
    owned_omega = lax.dynamic_slice_in_dim(omega_sq, start_owned, owned_count, 0)
    matrix = stiffness[None] + owned_omega[:, None, None] * identity[None] + coupling * owned_self
    owned_green = invert(matrix)
    rounded_all = gather_directly(owned_green.astype(jnp.bfloat16), "energy", 0)

    def add_term(running, paired):
        green_one, offset = paired
        window_part = lax.dynamic_slice_in_dim(sandwich_window, per_device - offset, per_device, 0)
        return (
            running + green_one.astype(jnp.float32)[None] * window_part.astype(jnp.float32),
            None,
        )

    mixture, unused = lax.scan(
        add_term, jnp.zeros((per_device, order, order), jnp.float32), (rounded_all, shifts)
    )
    mixture = mixture.astype(jnp.bfloat16)
    second = jnp.einsum(
        "ij,ejk->eik", layer_grad, mixture, preferred_element_type=jnp.float32
    ).astype(jnp.bfloat16)
    electron = jnp.einsum(
        "eij,kj->eik", second, layer_grad, preferred_element_type=jnp.float32
    ).astype(jnp.bfloat16)
    return (owned_self[:, None], owned_green[:, None], electron[:, None])


def solution(mesh):
    return jax.shard_map(
        body,
        mesh=mesh,
        in_specs=(
            P("energy", "layer", None, None),
            P("layer", None, None),
            P("layer", None, None),
            P("layer", None, None),
            P("layer", None, None),
            P(),
            P(),
        ),
        out_specs=(
            P("energy", "layer", None, None),
            P("energy", "layer", None, None),
            P("energy", "layer", None, None),
        ),
        check_vma=False,
    )
```

profile of v0, /device:TPU:34, one launch (start us, length us, event | category | flops | bytes accessed | tf_op | source)
XLA Modules:
  0.0 514.6 jit_solution(12438069681507777908)
XLA Ops:
  0.6 6.4 %copy.12 = bf16[32,1,256,256]{2,3,0,1:T(8,128)(2,1)} copy(bf16[32,1,256,256]{3,2,1,0:T(8,128)(2,1)} %param.11) | data formatting | bytes 8388608 | tf_op args[0]
  17.2 8.5 %fusion.3 = f32[32,256,256]{2,1,0:T(8,128)} fusion(bf16[1,256,256]{2,1,0:T(8,128)(2,1)S(1)} %copy-done, bf16[32,1,256,256]{3,2,1,0:T(8,128)(2,1)} %param.11), kind=kOutput, calls=%fused_computation.10 | convolution fusion | flops 2149580800 | bytes 12713984 | tf_op jit(solution)/shard_map/eij,kj->eik/dot_general | solution.py:77
  25.7 13.4 %collective-permute-done = bf16[32,128,128]{1,2,0:T(8,128)(2,1)S(1)} collective-permute-done((bf16[32,128,128]{1,2,0:T(8,128)(2,1)S(1)}, bf16[32,128,128]{1,2,0:T(8,128)(2,1)S(1)}, u32[]{:S(2)}, u32[]{:S(2)}) %collective-permute-start) | collective-permute-done | bytes 1048608 | tf_op jit(solution)/shard_map/ppermute | solution.py:17
  39.1 5.5 %fusion.21 = f32[32,256,256]{2,1,0:T(8,128)} fusion(bf16[32,128,128]{1,2,0:T(8,128)(2,1)S(1)} %collective-permute-done, bf16[1,256,128]{2,1,0:T(8,128)(2,1)S(1)} %copy-done.2), kind=kOutput, calls=%fused_computation.22 | convolution fusion | flops 806354944 | bytes 9502720 | tf_op jit(solution)/shard_map/eij,kj->eik/dot_general | solution.py:81
  44.6 16.4 %collective-permute-done.1 = bf16[32,128,128]{1,2,0:T(8,128)(2,1)} collective-permute-done((bf16[32,128,128]{1,2,0:T(8,128)(2,1)S(1)}, bf16[32,128,128]{1,2,0:T(8,128)(2,1)}, u32[]{:S(2)}, u32[]{:S(2)}) %collective-permute-start.1) | collective-permute-done | bytes 1048608 | tf_op jit(solution)/shard_map/ppermute | solution.py:17
  61.0 10.3 %add_convert_fusion = bf16[32,256,256]{2,1,0:T(8,128)(2,1)} fusion(f32[32,256,256]{2,1,0:T(8,128)} %fusion.3, f32[32,256,256]{2,1,0:T(8,128)} %fusion.21, bf16[32,128,128]{1,2,0:T(8,128)(2,1)} %collective-permute-done.1, bf16[1,256,128]{2,1,0:T(8,128)(2,1)S(1)} %copy-done.3), kind=kOutput, calls=%fused_computation.7 | convolution fusion | flops 812646400 | bytes 22085632 | tf_op jit(solution)/shard_map/eij,kj->eik/dot_general | solution.py:87
  73.2 50.3 %collective-permute-done.2 = bf16[32,256,256]{2,1,0:T(8,128)(2,1)} collective-permute-done((bf16[32,256,256]{2,1,0:T(8,128)(2,1)}, bf16[32,256,256]{2,1,0:T(8,128)(2,1)}, u32[]{:S(2)}, u32[]{:S(2)}) %collective-permute-start.2) | collective-permute-done | bytes 4194336 | tf_op jit(solution)/shard_map/ppermute | solution.py:17
  123.5 7.4 %pad_maximum_fusion = bf16[64,256,256]{2,1,0:T(8,128)(2,1)} fusion(bf16[32,256,256]{2,1,0:T(8,128)(2,1)} %add_convert_fusion, bf16[32,256,256]{2,1,0:T(8,128)(2,1)} %collective-permute-done.2), kind=kLoop, calls=%fused_computation.6 | loop fusion | flops 4194304 | bytes 16777216 | tf_op jit(solution)/shard_map/concatenate | solution.py:92
  130.9 118.0 %while.25 = (s32[]{:T(128)}, f32[16,256,256]{2,1,0:T(8,128)}, s32[16]{0:T(128)S(1)}, bf16[64,256,256]{2,1,0:T(8,128)(2,1)}, bf16[32,256,256]{2,1,0:T(8,128)(2,1)...) while((s32[]{:T(128)}, f32[16,256,256]{2,1,0:T(8,128)}, s32[16]{0:T(128)S(1)}, ...), condition=%wide.region_1.2_spmd, body=%wide.region_0.1_spmd.sunk | while | flops 8323078 | bytes 9175207 | solution.py:98
  169.7 4.8 fusion.60
  206.5 4.8 fusion.60
  257.5 26.5 %all-to-all-done = bf16[16,1,256,256]{3,2,1,0:T(8,128)(2,1)S(1)} async-done(((bf16[16,1,256,256]{3,2,1,0:T(8,128)(2,1)}), bf16[16,1,256,256]{3,2,1,0:T(8,128)(2,1)S(1)}, u32[]{:S(2)}, u32[]{:S(2)}) %all-to-all-start) | async-done | bytes 2097184 | tf_op jit(solution)/shard_map/all_to_all | solution.py:28
  292.0 7.2 %all-to-all-start.1 = ((bf16[16,1,256,256]{3,2,1,0:T(8,128)(2,1)}), bf16[16,1,256,256]{3,2,1,0:T(8,128)(2,1)S(1)}, u32[]{:S(2)}, u32[]{:S(2)}) async-start(bf16[16,1,256,256]{3,2,1,0:T(8,128)(2,1)} %broadcast_in_dim.38), calls=%async_computation.1 | async-start | bytes 4194304 | tf_op jit(solution)/shard_map/all_to_all | solution.py:40
  299.2 27.1 %all-to-all-done.1 = bf16[16,1,256,256]{3,2,1,0:T(8,128)(2,1)S(1)} async-done(((bf16[16,1,256,256]{3,2,1,0:T(8,128)(2,1)}), bf16[16,1,256,256]{3,2,1,0:T(8,128)(2,1)S(1)}, u32[]{:S(2)}, u32[]{:S(2)}) %all-to-all-start.1) | async-done | bytes 2097184 | tf_op jit(solution)/shard_map/all_to_all | solution.py:40
  326.3 179.7 %while.26 = (s32[]{:T(128)}, f32[32,256,256]{2,1,0:T(8,128)}, bf16[16,256,256]{2,1,0:T(8,128)(2,1)S(1)}, s32[16]{0:T(128)S(1)}, bf16[64,256,256]{2,1,0:T(8,128)(...) while((s32[]{:T(128)}, f32[32,256,256]{2,1,0:T(8,128)}, ...), condition=%wide.region_4.5_spmd.clone, body=%wide.region_3.4_spmd.clone.sunk | while | flops 8454151 | bytes 21627056 | solution.py:115
  328.2 7.1 %select_add_fusion.2 = f32[32,256,256]{2,1,0:T(8,128)} fusion(f32[32,256,256]{2,1,0:T(8,128)} %get-tuple-element.290, bf16[64,256,256]{2,1,0:T(8,128)(2,1)} %get-tuple-element.302, s32[]{:T(128)S(6)} %select_n.24, f32[256,256]{1,0:T(8,128)S(1)} %bitcast_convert_fusion.2, pred[]{:T(512)S(6)} %compare.3), kind=kLoop, calls=%fused_computation.1.clone.1 | loop fusion | flops 8388608 | bytes 21233668 | tf_op jit(solution)/shard_map/while/body/eval_jaxpr/add | solution.py:111
  337.2 9.5 %select_add_fusion.2 = f32[32,256,256]{2,1,0:T(8,128)} fusion(f32[32,256,256]{2,1,0:T(8,128)} %get-tuple-element.290, bf16[64,256,256]{2,1,0:T(8,128)(2,1)} %get-tuple-element.302, s32[]{:T(128)S(6)} %select_n.24, f32[256,256]{1,0:T(8,128)S(1)} %bitcast_convert_fusion.2, pred[]{:T(512)S(6)} %compare.3), kind=kLoop, calls=%fused_computation.1.clone.1 | loop fusion | flops 8388608 | bytes 21233668 | tf_op jit(solution)/shard_map/while/body/eval_jaxpr/add | solution.py:111
  348.6 9.5 %select_add_fusion.2 = f32[32,256,256]{2,1,0:T(8,128)} fusion(f32[32,256,256]{2,1,0:T(8,128)} %get-tuple-element.290, bf16[64,256,256]{2,1,0:T(8,128)(2,1)} %get-tuple-element.302, s32[]{:T(128)S(6)} %select_n.24, f32[256,256]{1,0:T(8,128)S(1)} %bitcast_convert_fusion.2, pred[]{:T(512)S(6)} %compare.3), kind=kLoop, calls=%fused_computation.1.clone.1 | loop fusion | flops 8388608 | bytes 21233668 | tf_op jit(solution)/shard_map/while/body/eval_jaxpr/add | solution.py:111
  360.0 9.5 %select_add_fusion.2 = f32[32,256,256]{2,1,0:T(8,128)} fusion(f32[32,256,256]{2,1,0:T(8,128)} %get-tuple-element.290, bf16[64,256,256]{2,1,0:T(8,128)(2,1)} %get-tuple-element.302, s32[]{:T(128)S(6)} %select_n.24, f32[256,256]{1,0:T(8,128)S(1)} %bitcast_convert_fusion.2, pred[]{:T(512)S(6)} %compare.3), kind=kLoop, calls=%fused_computation.1.clone.1 | loop fusion | flops 8388608 | bytes 21233668 | tf_op jit(solution)/shard_map/while/body/eval_jaxpr/add | solution.py:111
  371.4 9.5 %select_add_fusion.2 = f32[32,256,256]{2,1,0:T(8,128)} fusion(f32[32,256,256]{2,1,0:T(8,128)} %get-tuple-element.290, bf16[64,256,256]{2,1,0:T(8,128)(2,1)} %get-tuple-element.302, s32[]{:T(128)S(6)} %select_n.24, f32[256,256]{1,0:T(8,128)S(1)} %bitcast_convert_fusion.2, pred[]{:T(512)S(6)} %compare.3), kind=kLoop, calls=%fused_computation.1.clone.1 | loop fusion | flops 8388608 | bytes 21233668 | tf_op jit(solution)/shard_map/while/body/eval_jaxpr/add | solution.py:111
  382.7 9.5 %select_add_fusion.2 = f32[32,256,256]{2,1,0:T(8,128)} fusion(f32[32,256,256]{2,1,0:T(8,128)} %get-tuple-element.290, bf16[64,256,256]{2,1,0:T(8,128)(2,1)} %get-tuple-element.302, s32[]{:T(128)S(6)} %select_n.24, f32[256,256]{1,0:T(8,128)S(1)} %bitcast_convert_fusion.2, pred[]{:T(512)S(6)} %compare.3), kind=kLoop, calls=%fused_computation.1.clone.1 | loop fusion | flops 8388608 | bytes 21233668 | tf_op jit(solution)/shard_map/while/body/eval_jaxpr/add | solution.py:111
  394.1 9.5 %select_add_fusion.2 = f32[32,256,256]{2,1,0:T(8,128)} fusion(f32[32,256,256]{2,1,0:T(8,128)} %get-tuple-element.290, bf16[64,256,256]{2,1,0:T(8,128)(2,1)} %get-tuple-element.302, s32[]{:T(128)S(6)} %select_n.24, f32[256,256]{1,0:T(8,128)S(1)} %bitcast_convert_fusion.2, pred[]{:T(512)S(6)} %compare.3), kind=kLoop, calls=%fused_computation.1.clone.1 | loop fusion | flops 8388608 | bytes 21233668 | tf_op jit(solution)/shard_map/while/body/eval_jaxpr/add | solution.py:111
  405.5 9.5 %select_add_fusion.2 = f32[32,256,256]{2,1,0:T(8,128)} fusion(f32[32,256,256]{2,1,0:T(8,128)} %get-tuple-element.290, bf16[64,256,256]{2,1,0:T(8,128)(2,1)} %get-tuple-element.302, s32[]{:T(128)S(6)} %select_n.24, f32[256,256]{1,0:T(8,128)S(1)} %bitcast_convert_fusion.2, pred[]{:T(512)S(6)} %compare.3), kind=kLoop, calls=%fused_computation.1.clone.1 | loop fusion | flops 8388608 | bytes 21233668 | tf_op jit(solution)/shard_map/while/body/eval_jaxpr/add | solution.py:111
  416.9 9.5 %select_add_fusion.2 = f32[32,256,256]{2,1,0:T(8,128)} fusion(f32[32,256,256]{2,1,0:T(8,128)} %get-tuple-element.290, bf16[64,256,256]{2,1,0:T(8,128)(2,1)} %get-tuple-element.302, s32[]{:T(128)S(6)} %select_n.24, f32[256,256]{1,0:T(8,128)S(1)} %bitcast_convert_fusion.2, pred[]{:T(512)S(6)} %compare.3), kind=kLoop, calls=%fused_computation.1.clone.1 | loop fusion | flops 8388608 | bytes 21233668 | tf_op jit(solution)/shard_map/while/body/eval_jaxpr/add | solution.py:111
  428.3 9.5 %select_add_fusion.2 = f32[32,256,256]{2,1,0:T(8,128)} fusion(f32[32,256,256]{2,1,0:T(8,128)} %get-tuple-element.290, bf16[64,256,256]{2,1,0:T(8,128)(2,1)} %get-tuple-element.302, s32[]{:T(128)S(6)} %select_n.24, f32[256,256]{1,0:T(8,128)S(1)} %bitcast_convert_fusion.2, pred[]{:T(512)S(6)} %compare.3), kind=kLoop, calls=%fused_computation.1.clone.1 | loop fusion | flops 8388608 | bytes 21233668 | tf_op jit(solution)/shard_map/while/body/eval_jaxpr/add | solution.py:111
  439.7 9.5 %select_add_fusion.2 = f32[32,256,256]{2,1,0:T(8,128)} fusion(f32[32,256,256]{2,1,0:T(8,128)} %get-tuple-element.290, bf16[64,256,256]{2,1,0:T(8,128)(2,1)} %get-tuple-element.302, s32[]{:T(128)S(6)} %select_n.24, f32[256,256]{1,0:T(8,128)S(1)} %bitcast_convert_fusion.2, pred[]{:T(512)S(6)} %compare.3), kind=kLoop, calls=%fused_computation.1.clone.1 | loop fusion | flops 8388608 | bytes 21233668 | tf_op jit(solution)/shard_map/while/body/eval_jaxpr/add | solution.py:111
  451.0 9.5 %select_add_fusion.2 = f32[32,256,256]{2,1,0:T(8,128)} fusion(f32[32,256,256]{2,1,0:T(8,128)} %get-tuple-element.290, bf16[64,256,256]{2,1,0:T(8,128)(2,1)} %get-tuple-element.302, s32[]{:T(128)S(6)} %select_n.24, f32[256,256]{1,0:T(8,128)S(1)} %bitcast_convert_fusion.2, pred[]{:T(512)S(6)} %compare.3), kind=kLoop, calls=%fused_computation.1.clone.1 | loop fusion | flops 8388608 | bytes 21233668 | tf_op jit(solution)/shard_map/while/body/eval_jaxpr/add | solution.py:111
  462.4 9.5 %select_add_fusion.2 = f32[32,256,256]{2,1,0:T(8,128)} fusion(f32[32,256,256]{2,1,0:T(8,128)} %get-tuple-element.290, bf16[64,256,256]{2,1,0:T(8,128)(2,1)} %get-tuple-element.302, s32[]{:T(128)S(6)} %select_n.24, f32[256,256]{1,0:T(8,128)S(1)} %bitcast_convert_fusion.2, pred[]{:T(512)S(6)} %compare.3), kind=kLoop, calls=%fused_computation.1.clone.1 | loop fusion | flops 8388608 | bytes 21233668 | tf_op jit(solution)/shard_map/while/body/eval_jaxpr/add | solution.py:111
  473.8 9.5 %select_add_fusion.2 = f32[32,256,256]{2,1,0:T(8,128)} fusion(f32[32,256,256]{2,1,0:T(8,128)} %get-tuple-element.290, bf16[64,256,256]{2,1,0:T(8,128)(2,1)} %get-tuple-element.302, s32[]{:T(128)S(6)} %select_n.24, f32[256,256]{1,0:T(8,128)S(1)} %bitcast_convert_fusion.2, pred[]{:T(512)S(6)} %compare.3), kind=kLoop, calls=%fused_computation.1.clone.1 | loop fusion | flops 8388608 | bytes 21233668 | tf_op jit(solution)/shard_map/while/body/eval_jaxpr/add | solution.py:111
  485.2 9.5 %select_add_fusion.2 = f32[32,256,256]{2,1,0:T(8,128)} fusion(f32[32,256,256]{2,1,0:T(8,128)} %get-tuple-element.290, bf16[64,256,256]{2,1,0:T(8,128)(2,1)} %get-tuple-element.302, s32[]{:T(128)S(6)} %select_n.24, f32[256,256]{1,0:T(8,128)S(1)} %bitcast_convert_fusion.2, pred[]{:T(512)S(6)} %compare.3), kind=kLoop, calls=%fused_computation.1.clone.1 | loop fusion | flops 8388608 | bytes 21233668 | tf_op jit(solution)/shard_map/while/body/eval_jaxpr/add | solution.py:111
  496.6 9.5 %select_add_fusion.2 = f32[32,256,256]{2,1,0:T(8,128)} fusion(f32[32,256,256]{2,1,0:T(8,128)} %get-tuple-element.290, bf16[64,256,256]{2,1,0:T(8,128)(2,1)} %get-tuple-element.302, s32[]{:T(128)S(6)} %select_n.24, f32[256,256]{1,0:T(8,128)S(1)} %bitcast_convert_fusion.2, pred[]{:T(512)S(6)} %compare.3), kind=kLoop, calls=%fused_computation.1.clone.1 | loop fusion | flops 8388608 | bytes 21233668 | tf_op jit(solution)/shard_map/while/body/eval_jaxpr/add | solution.py:111
  506.0 8.5 %convert_bitcast_fusion = bf16[32,1,256,256]{3,2,1,0:T(8,128)(2,1)} fusion(f32[32,256,256]{2,1,0:T(8,128)} %get-tuple-element.134, bf16[1,256,256]{2,1,0:T(8,128)(2,1)S(1)} %copy-done), kind=kOutput, calls=%fused_computation.12 | convolution fusion | flops 2153775104 | bytes 12713984 | tf_op jit(solution)/shard_map/eij,kj->eik/dot_general | solution.py:122
  (112 shorter events, 125.8 us)
Async XLA Ops:
  0.6 16.6 %copy-start = (bf16[1,256,256]{2,1,0:T(8,128)(2,1)S(1)}, bf16[1,256,256]{2,1,0:T(8,128)(2,1)}, u32[]{:S(2)}) copy-start(bf16[1,256,256]{2,1,0:T(8,128)(2,1)} %param.12) | copy-start | bytes 393220
  8.8 30.3 %collective-permute-start = (bf16[32,128,128]{1,2,0:T(8,128)(2,1)S(1)}, bf16[32,128,128]{1,2,0:T(8,128)(2,1)S(1)}, u32[]{:S(2)}, u32[]{:S(2)}) collective-permute-start(bf16[32,128,128]{1,2,0:T(8,128)(2,1)S(1)} %get-tuple-element.188), channel_id=1, source_target_pairs={{0,1},{1,2},{2,3},{3,4},{4,5},{5,6},{6,7},{8,9},{9,10},{10,11},{11... | collective-permute-start | bytes 3145736 | tf_op jit(solution)/shard_map/ppermute | solution.py:17
  12.8 26.3 %copy-start.2 = (bf16[1,256,128]{2,1,0:T(8,128)(2,1)S(1)}, bf16[1,256,128]{2,1,0:T(8,128)(2,1)}, u32[]{:S(2)}) copy-start(bf16[1,256,128]{2,1,0:T(8,128)(2,1)} %param.13) | copy-start | bytes 196612
  12.8 48.2 %collective-permute-start.1 = (bf16[32,128,128]{1,2,0:T(8,128)(2,1)S(1)}, bf16[32,128,128]{1,2,0:T(8,128)(2,1)}, u32[]{:S(2)}, u32[]{:S(2)}) collective-permute-start(bf16[32,128,128]{1,2,0:T(8,128)(2,1)S(1)} %get-tuple-element.187), channel_id=1, source_target_pairs={{1,0},{2,1},{3,2},{4,3},{5,4},{6,5},{7,6},{9,8},{10,9},{11,10},{12... | collective-permute-start | bytes 3145736 | tf_op jit(solution)/shard_map/ppermute | solution.py:17
  25.7 35.3 %copy-start.3 = (bf16[1,256,128]{2,1,0:T(8,128)(2,1)S(1)}, bf16[1,256,128]{2,1,0:T(8,128)(2,1)}, u32[]{:S(2)}) copy-start(bf16[1,256,128]{2,1,0:T(8,128)(2,1)} %param.14) | copy-start | bytes 196612
  71.3 52.2 %collective-permute-start.2 = (bf16[32,256,256]{2,1,0:T(8,128)(2,1)}, bf16[32,256,256]{2,1,0:T(8,128)(2,1)}, u32[]{:S(2)}, u32[]{:S(2)}) collective-permute-start(bf16[32,256,256]{2,1,0:T(8,128)(2,1)} %add_convert_fusion), channel_id=1, source_target_pairs={{0,8},{8,16},{16,24},{24,32},{32,40},{40,48},{48,56},{56,64},{64,7... | collective-permute-start | bytes 12582920 | tf_op jit(solution)/shard_map/ppermute | solution.py:17
  73.2 57.7 %copy-start.6 = (s32[16]{0:T(128)S(1)}, s32[16]{0:T(128)}, u32[]{:S(2)}) copy-start(s32[16]{0:T(128)} %param.17) | copy-start | bytes 196
  248.9 8.1 %copy-start.5 = (f32[16]{0:T(128)S(1)}, f32[16]{0:T(128)}, u32[]{:S(2)}) copy-start(f32[16]{0:T(128)} %param.16) | copy-start | bytes 196
  253.0 31.4 %copy-start.4 = (f32[1,256,256]{2,1,0:T(8,128)S(1)}, f32[1,256,256]{2,1,0:T(8,128)}, u32[]{:S(2)}) copy-start(f32[1,256,256]{2,1,0:T(8,128)} %param.15) | copy-start | bytes 786436
  253.0 31.1 %all-to-all-start = ((bf16[16,1,256,256]{3,2,1,0:T(8,128)(2,1)}), bf16[16,1,256,256]{3,2,1,0:T(8,128)(2,1)S(1)}, u32[]{:S(2)}, u32[]{:S(2)}) async-start(bf16[16,1,256,256]{3,2,1,0:T(8,128)(2,1)} %fusion.19), calls=%async_computation | async-start | bytes 4194304 | tf_op jit(solution)/shard_map/all_to_all | solution.py:28
  284.3 7.7 %copy-start.1 = (f32[256,256]{1,0:T(8,128)}, f32[256,256]{1,0:T(8,128)S(1)}, u32[]{:S(2)}) copy-start(f32[256,256]{1,0:T(8,128)S(1)} %convert_reduce_fusion) | copy-start | bytes 786436
  292.0 34.3 %all-to-all-start.1 = ((bf16[16,1,256,256]{3,2,1,0:T(8,128)(2,1)}), bf16[16,1,256,256]{3,2,1,0:T(8,128)(2,1)S(1)}, u32[]{:S(2)}, u32[]{:S(2)}) async-start(bf16[16,1,256,256]{3,2,1,0:T(8,128)(2,1)} %broadcast_in_dim.38), calls=%async_computation.1 | async-start | bytes 4194304 | tf_op jit(solution)/shard_map/all_to_all | solution.py:40
where the time goes:
time: 518 us; the launch traced here: 515 us
  other arithmetic  238 us (46%)
  waiting for transfers between devices  134 us (26%)
  local copies, waits for them, and re-layouts  42.9 us (8%)
  loops' own time  41.9 us (8%)
  matrix products  35.8 us (7%)
  starting transfers between devices  21.4 us (4%)
    add x16, other arithmetic, add_term(): running + green_one.astype(jnp.float32)[None] * window_part.astype(jnp.fl...  149 us
    ppermute x3, waiting for transfers between devices, shifted(): lax.ppermute(value, axis, [(source, source + steps) for source in range(l...  80.1 us
    dot_general x16, other arithmetic, phonon_term(): jnp.einsum('ern,ern->rn', window_part, blocks, preferred_element_type=jnp...  76.1 us
    all_to_all x1, waiting for transfers between devices, copy_for_each(): return lax.all_to_all(copies, axis, split_axis=0, concat_axis=0, tiled=True)  27.1 us
    all_to_all x1, waiting for transfers between devices, sent_and_summed(): lax.all_to_all(tiles, axis, split_axis=0, concat_axis=0, tiled=True)  26.5 us
    another operation x1, loops' own time, body(): lax.scan(add_term, jnp.zeros((per_device, order, order), jnp.float32), (r...  21 us
    another operation x1, loops' own time, body(): partial_self = lax.map(phonon_term, shifts) * scale  21 us
    dynamic_slice x32, local copies, waits for them, and re-layouts, body(): partial_self = lax.map(phonon_term, shifts) * scale  18.6 us
  transfers between devices with their start and end apart: 5, of which 5 were waited for; matrix products, arithmetic and copies ran while one was open for 3% of the time, Pallas kernels for 0%

commit v1 on v0

v1 whole, which is shorter than its diff:
```python
import functools
import math

import jax
import jax.numpy as jnp
from jax import lax
from jax.experimental import pallas as pl
from jax.experimental.pallas import tpu as pltpu
from jax.sharding import PartitionSpec as P

NEWTON = 3
COUPLING = 0.01
MESH = pl.DeviceIdType.MESH
BF = jnp.bfloat16
F32 = jnp.float32

PER = 32
NB = 256
HALF = 128
CH = 4
STEPS = PER // CH
AHEAD = 2
W = 16
CHIPS = 8
ROWS = 32


def nn(a, b, **kw):
    return lax.dot_general(a, b, (((1,), (0,)), ((), ())), preferred_element_type=F32, **kw)


def nt(a, b, **kw):
    return lax.dot_general(a, b, (((1,), (1,)), ((), ())), preferred_element_type=F32, **kw)


def tree(terms):
    while len(terms) > 1:
        terms = [terms[i] + terms[i + 1] if i + 1 < len(terms) else terms[i] for i in range(0, len(terms), 2)]
    return terms[0]


def scatter_kernel(
    scale, shifts, omega, green, grad, left_cpl, right_cpl, stiff,
    self_out, green_out, turned_out,
    gpad, win, left_in, right_in, first, acc, part, sums, from_core, from_chip, rounded, mix, tile, turned,
    g_sem, ls, lr, rs, rr, us, ur, c1s, c1r, c2s, c2r, gs, gr, fs, fr, ts,
):
    me = lax.axis_index("energy")
    layer = lax.axis_index("layer")
    core = lax.rem(me, 2)
    chip = me // 2
    has_lower, has_upper = me > 0, me < 15
    has_left, has_right = layer > 0, layer < 7
    partner = {"energy": me + 1 - 2 * core, "layer": layer}

    def g_copy(c):
        return pltpu.make_async_copy(
            green.at[pl.ds(c * CH, CH)], gpad.at[pl.ds(PER + c * CH, CH)], g_sem.at[c])

    def left_copy(c):
        return pltpu.make_async_remote_copy(
            src_ref=green.at[pl.ds(c * CH, CH), pl.ds(HALF, HALF), pl.ds(HALF, HALF)],
            dst_ref=left_in.at[pl.ds(c * CH, CH)], send_sem=ls.at[c], recv_sem=lr.at[c],
            device_id={"energy": me, "layer": lax.rem(layer + 1, 8)}, device_id_type=MESH)

    def right_copy(c):
        return pltpu.make_async_remote_copy(
            src_ref=green.at[pl.ds(c * CH, CH), pl.ds(0, HALF), pl.ds(0, HALF)],
            dst_ref=right_in.at[pl.ds(c * CH, CH)], send_sem=rs.at[c], recv_sem=rr.at[c],
            device_id={"energy": me, "layer": lax.rem(layer + 7, 8)}, device_id_type=MESH)

    def up_copy(c):
        return pltpu.make_async_remote_copy(
            src_ref=win.at[pl.ds(PER + c * CH, CH)], dst_ref=win.at[pl.ds(c * CH, CH)],
            send_sem=us.at[c], recv_sem=ur.at[c],
            device_id={"energy": lax.rem(me + 1, 16), "layer": layer}, device_id_type=MESH)

    def start_surfaces(c):
        @pl.when(has_right)
        def _():
            left_copy(c).start()

        @pl.when(has_left)
        def _():
            right_copy(c).start()

    for c in range(STEPS):
        g_copy(c).start()

    barrier = pltpu.get_barrier_semaphore()
    for k in range(1, 16):
        pl.semaphore_signal(
            barrier, inc=1, device_id={"energy": lax.rem(me + k, 16), "layer": layer}, device_id_type=MESH)

    @pl.when(has_right)
    def _():
        pl.semaphore_signal(barrier, inc=1, device_id={"energy": me, "layer": layer + 1}, device_id_type=MESH)

    @pl.when(has_left)
    def _():
        pl.semaphore_signal(barrier, inc=1, device_id={"energy": me, "layer": layer - 1}, device_id_type=MESH)

    pl.semaphore_wait(barrier, 15 + has_left.astype(jnp.int32) + has_right.astype(jnp.int32))

    for c in range(AHEAD):
        start_surfaces(c)

    def clear(i, carry):
        zero = jnp.zeros((NB, NB), BF)
        gpad[i] = zero
        gpad[2 * PER + i] = zero
        return carry

    lax.fori_loop(0, PER, clear, 0)

    @pl.when(jnp.logical_not(has_lower))
    def _():
        def fill(i, carry):
            win[i] = jnp.zeros((NB, NB), BF)
            return carry

        lax.fori_loop(0, PER, fill, 0)

    @pl.when(jnp.logical_not(has_left))
    def _():
        def fill(i, carry):
            left_in[i] = jnp.zeros((HALF, HALF), BF)
            return carry

        lax.fori_loop(0, PER, fill, 0)

    @pl.when(jnp.logical_not(has_right))
    def _():
        def fill(i, carry):
            right_in[i] = jnp.zeros((HALF, HALF), BF)
            return carry

        lax.fori_loop(0, PER, fill, 0)

    def clear_acc(w, carry):
        acc[w] = jnp.zeros((NB, NB), F32)
        return carry

    lax.fori_loop(0, W, clear_acc, 0)

    for c in range(STEPS):
        g_copy(c).wait()

    def correlate(s_base, g_base):
        def one(t, carry):
            rows = pl.ds(pl.multiple_of(t * ROWS, ROWS), ROWS)
            held = [win[s_base + i, rows, :] for i in range(CH)]
            for w in range(W):
                at = g_base + shifts[w]
                terms = [held[i] * gpad[at + i, rows, :] for i in range(CH)]
                acc[w, rows, :] += tree(terms).astype(F32)
            return carry

        lax.fori_loop(0, NB // ROWS, one, 0)

    a = grad[...]
    lc = left_cpl[...]
    rc = right_cpl[...]

    def step(c, carry):
        e0 = c * CH
        for i in range(CH):
            first[pl.ds(i * NB, NB), :] = nn(a, gpad[PER + e0 + i]).astype(BF)

        @pl.when(has_left)
        def _():
            left_copy(c).wait_recv()

        @pl.when(has_right)
        def _():
            right_copy(c).wait_recv()

        lp = [nn(lc, left_in[e0 + i]).astype(BF) for i in range(CH)]
        rp = [nn(rc, right_in[e0 + i]).astype(BF) for i in range(CH)]
        for i in range(CH):
            total = nt(first[pl.ds(i * NB, NB), :], a) + nt(lp[i], lc) + nt(rp[i], rc)
            win[PER + e0 + i] = total.astype(BF)

        @pl.when(has_upper)
        def _():
            up_copy(c).start()

        @pl.when(has_right)
        def _():
            left_copy(c).wait_send()

        @pl.when(has_left)
        def _():
            right_copy(c).wait_send()

        @pl.when(c + AHEAD < STEPS)
        def _():
            start_surfaces(c + AHEAD)

        correlate(PER + e0, PER + e0)

        @pl.when(c > 0)
        def _():
            @pl.when(has_lower)
            def _():
                up_copy(c - 1).wait_recv()

            correlate(e0 - CH, e0 - CH)

        return carry

    lax.fori_loop(0, STEPS, step, 0)

    def core_copy(j):
        return pltpu.make_async_remote_copy(
            src_ref=part.at[j], dst_ref=from_core.at[j], send_sem=c1s.at[j], recv_sem=c1r.at[j],
            device_id=partner, device_id_type=MESH)

    last = PER - CH

    @pl.when(has_lower)
    def _():
        up_copy(STEPS - 1).wait_recv()

    def finish(w, store):
        at = last + shifts[w]

        def one(t, carry):
            rows = pl.ds(pl.multiple_of(t * ROWS, ROWS), ROWS)
            terms = [win[last + i, rows, :] * gpad[at + i, rows, :] for i in range(CH)]
            store(rows, (acc[w, rows, :] + tree(terms).astype(F32)) * scale)
            return carry

        lax.fori_loop(0, NB // ROWS, one, 0)

    def theirs(k, carry):
        j = lax.rem(chip + k, CHIPS)

        def store(rows, value):
            part[j, rows, :] = value.astype(BF)

        finish(2 * j + 1 - core, store)
        core_copy(j).start()
        return carry

    lax.fori_loop(1, CHIPS + 1, theirs, 0)

    def ours(k, carry):
        j = lax.rem(chip + k, CHIPS)
        w = 2 * j + core

        def store(rows, value):
            acc[w, rows, :] = value

        finish(w, store)
        return carry

    lax.fori_loop(1, CHIPS + 1, ours, 0)

    def chip_copy(k):
        return pltpu.make_async_remote_copy(
            src_ref=sums.at[k - 1], dst_ref=from_chip.at[k - 1], send_sem=c2s.at[k - 1], recv_sem=c2r.at[k - 1],
            device_id={"energy": 2 * lax.rem(chip + k, CHIPS) + core, "layer": layer}, device_id_type=MESH)

    def join(k, carry):
        j = lax.rem(chip + k, CHIPS)
        w = 2 * j + core
        core_copy(j).wait_recv()

        def one(t, c2):
            rows = pl.ds(pl.multiple_of(t * ROWS, ROWS), ROWS)
            sums[k - 1, rows, :] = (acc[w, rows, :] + from_core[j, rows, :].astype(F32)).astype(BF)
            return c2

        lax.fori_loop(0, NB // ROWS, one, 0)
        chip_copy(k).start()
        return carry

    lax.fori_loop(1, CHIPS, join, 0)
    core_copy(chip).wait_recv()
    for k in range(1, CHIPS):
        chip_copy(k).wait_recv()

    def total_rows(t, carry):
        rows = pl.ds(pl.multiple_of(t * ROWS, ROWS), ROWS)
        value = acc[me, rows, :] + from_core[chip, rows, :].astype(F32)
        for k in range(CHIPS - 1):
            value = value + from_chip[k, rows, :].astype(F32)
        self_out[rows, :] = value
        return carry

    lax.fori_loop(0, NB // ROWS, total_rows, 0)

    on_diag = lax.broadcasted_iota(jnp.int32, (NB, NB), 0) == lax.broadcasted_iota(jnp.int32, (NB, NB), 1)
    matrix = stiff[...] + COUPLING * self_out[...]
    matrix = matrix + jnp.where(on_diag, omega[me], 0.0)
    diag = jnp.where(on_diag, matrix, 0.0)
    inv_row = 1.0 / jnp.sum(diag, axis=0, keepdims=True)
    inv_col = 1.0 / jnp.sum(diag, axis=1, keepdims=True)
    approx = jnp.where(on_diag, 2.0 * inv_col, 0.0) - inv_col * (matrix * inv_row)
    for _ in range(NEWTON - 1):
        product = nn(matrix, approx, precision=lax.Precision.HIGHEST)
        approx = 2.0 * approx - nn(approx, product, precision=lax.Precision.HIGHEST)
    green_out[...] = approx
    rounded[me] = approx.astype(BF)

    def gather_copy(k):
        return pltpu.make_async_remote_copy(
            src_ref=rounded.at[me], dst_ref=rounded.at[me], send_sem=gs.at[k - 1], recv_sem=gr.at[k - 1],
            device_id={"energy": 2 * lax.rem(chip + k, CHIPS) + core, "layer": layer}, device_id_type=MESH)

    def gather_arrival(k):
        w = 2 * lax.rem(chip + CHIPS - k, CHIPS) + core
        return pltpu.make_async_remote_copy(
            src_ref=rounded.at[w], dst_ref=rounded.at[w], send_sem=gs.at[k - 1], recv_sem=gr.at[k - 1],
            device_id={"energy": w, "layer": layer}, device_id_type=MESH)

    def pass_on(k, whose):
        w = 2 * lax.rem(chip + CHIPS - k, CHIPS) + whose
        return pltpu.make_async_remote_copy(
            src_ref=rounded.at[w], dst_ref=rounded.at[w], send_sem=fs.at[k], recv_sem=fr.at[k],
            device_id=partner, device_id_type=MESH)

    pass_on(0, core).start()
    for k in range(1, CHIPS):
        gather_copy(k).start()

    group = 4
    for g in range(W // group):
        ws = []
        for k in (2 * g, 2 * g + 1):
            if k > 0:
                gather_arrival(k).wait_recv()
                pass_on(k, core).start()
        for k in (2 * g, 2 * g + 1):
            pass_on(k, 1 - core).wait_recv()
            owner = 2 * lax.rem(chip + CHIPS - k, CHIPS)
            ws += [owner, owner + 1]
        final = g == W // group - 1

        def mix_rows(t, carry):
            rows = pl.ds(pl.multiple_of(t * ROWS, ROWS), ROWS)
            held = [rounded[w, rows, :] for w in ws]
            ats = [PER - shifts[w] for w in ws]
            for e in range(PER):
                terms = [held[i] * win[ats[i] + e, rows, :] for i in range(group)]
                value = tree(terms).astype(F32)
                if g > 0:
                    value = mix[e, rows, :] + value
                if final:
                    tile[pl.ds(e * ROWS, ROWS), :] = value.astype(BF)
                else:
                    mix[e, rows, :] = value
            if final:
                out = nt(tile[...], a).astype(BF)
                for e in range(PER):
                    turned[e, rows, :] = out[e * ROWS:(e + 1) * ROWS]
                turn_copy(t).start()
            return carry

        def turn_copy(t):
            rows = pl.ds(pl.multiple_of(t * ROWS, ROWS), ROWS)
            return pltpu.make_async_copy(turned.at[:, rows, :], turned_out.at[:, rows, :], ts.at[t])

        lax.fori_loop(0, NB // ROWS, mix_rows, 0)

    for t in range(NB // ROWS):
        turn_copy(t).wait()
    for c in range(STEPS):
        @pl.when(has_upper)
        def _():
            up_copy(c).wait_send()
    for j in range(CHIPS):
        core_copy(j).wait_send()
        pass_on(j, core).wait_send()
    for k in range(1, CHIPS):
        chip_copy(k).wait_send()
        gather_copy(k).wait_send()


def last_kernel(grad, turned, out):
    a = grad[...]
    for i in range(out.shape[0]):
        out[i] = nn(a, turned[i]).astype(BF)


def body(green, gradient, left_coupling, right_coupling, dynamical, omega_sq, shifts):
    scale = 1.0 / math.sqrt(PER * lax.axis_size("energy"))
    vmem = pl.BlockSpec(memory_space=pltpu.VMEM)
    smem = pl.BlockSpec(memory_space=pltpu.SMEM)
    hbm = pl.BlockSpec(memory_space=pl.ANY)
    dma = pltpu.SemaphoreType.DMA
    own_self, own_green, turned = pl.pallas_call(
        functools.partial(scatter_kernel, scale),
        out_shape=[
            jax.ShapeDtypeStruct((NB, NB), F32),
            jax.ShapeDtypeStruct((NB, NB), F32),
            jax.ShapeDtypeStruct((PER, NB, NB), BF),
        ],
        in_specs=[smem, smem, hbm, vmem, vmem, vmem, vmem],
        out_specs=[vmem, vmem, hbm],
        scratch_shapes=[
            pltpu.VMEM((3 * PER, NB, NB), BF),
            pltpu.VMEM((2 * PER, NB, NB), BF),
            pltpu.VMEM((PER, HALF, HALF), BF),
            pltpu.VMEM((PER, HALF, HALF), BF),
            pltpu.VMEM((CH * NB, NB), BF),
            pltpu.VMEM((W, NB, NB), F32),
            pltpu.VMEM((CHIPS, NB, NB), BF),
            pltpu.VMEM((CHIPS - 1, NB, NB), BF),
            pltpu.VMEM((CHIPS, NB, NB), BF),
            pltpu.VMEM((CHIPS - 1, NB, NB), BF),
            pltpu.VMEM((W, NB, NB), BF),
            pltpu.VMEM((PER, NB, NB), F32),
            pltpu.VMEM((PER * ROWS, NB), BF),
            pltpu.VMEM((PER, NB, NB), BF),
            dma((STEPS,)),
            dma((STEPS,)), dma((STEPS,)), dma((STEPS,)), dma((STEPS,)), dma((STEPS,)), dma((STEPS,)),
            dma((CHIPS,)), dma((CHIPS,)), dma((CHIPS - 1,)), dma((CHIPS - 1,)),
            dma((CHIPS - 1,)), dma((CHIPS - 1,)), dma((CHIPS,)), dma((CHIPS,)),
            dma((NB // ROWS,)),
        ],
        compiler_params=pltpu.CompilerParams(
            collective_id=0, has_side_effects=True, vmem_limit_bytes=58 << 20),
        name="scatter",
    )(shifts, omega_sq, green[:, 0], gradient[0], left_coupling[0], right_coupling[0], dynamical[0])
    block = pl.BlockSpec((4, NB, NB), lambda i: (i, 0, 0))
    electron = pl.pallas_call(
        last_kernel,
        grid=(PER // 4,),
        in_specs=[pl.BlockSpec((NB, NB), lambda i: (0, 0)), block],
        out_specs=block,
        out_shape=jax.ShapeDtypeStruct((PER, NB, NB), BF),
        name="last",
    )(gradient[0], turned)
    return own_self[None, None], own_green[None, None], electron[:, None]


def solution(mesh):
    return jax.shard_map(
        body,
        mesh=mesh,
        in_specs=(
            P("energy", "layer", None, None),
            P("layer", None, None),
            P("layer", None, None),
            P("layer", None, None),
            P("layer", None, None),
            P(),
            P(),
        ),
        out_specs=(
            P("energy", "layer", None, None),
            P("energy", "layer", None, None),
            P("energy", "layer", None, None),
        ),
        check_vma=False,
    )
```

time: 518 us -> 160 us (0.31)
  other arithmetic: 238 us -> 0 us
  Pallas kernels: 0 us -> 155 us
  waiting for transfers between devices: 134 us -> 0 us
  loops' own time: 41.9 us -> 0 us
  local copies, waits for them, and re-layouts: 42.9 us -> 1.41 us
  matrix products: 35.8 us -> 0 us
  starting transfers between devices: 21.4 us -> 0 us
    pallas_call x0 -> x2, Pallas kernels: none -> 155 us  [the longest x1 147 us: body(): pl.pallas_call(functools.partial(scatter_kernel, scale), out_shape=[jax.S...]
    add x17 -> x0, other arithmetic: 150 us -> none  [the longest x16 149 us: add_term(): running + green_one.astype(jnp.float32)[None] * window_part.astype(jnp.fl...]
    ppermute x3 -> x0, waiting for transfers between devices: 80.1 us -> none  [shifted(): lax.ppermute(value, axis, [(source, source + steps) for source in range(l...]
    dot_general x16 -> x0, other arithmetic: 76.1 us -> none  [phonon_term(): jnp.einsum('ern,ern->rn', window_part, blocks, preferred_element_type=jnp...]
    all_to_all x2 -> x0, waiting for transfers between devices: 53.6 us -> none  [the longest x1 27.1 us: copy_for_each(): return lax.all_to_all(copies, axis, split_axis=0, concat_axis=0, tiled=True)]
    another operation x2 -> x0, loops' own time: 41.9 us -> none  [the longest x1 21 us: body(): lax.scan(add_term, jnp.zeros((per_device, order, order), jnp.float32), (r...]
    dot_general x10 -> x0, matrix products: 35.8 us -> none  [the longest x1 10.3 us: body(): jnp.einsum('eij,kj->eik', right_part, right_cpl, preferred_element_type=j...]
    dynamic_slice x33 -> x0, local copies, waits for them, and re-layouts: 19.2 us -> none  [the longest x32 18.6 us: body(): partial_self = lax.map(phonon_term, shifts) * scale]
  transfers between devices with their start and end apart: 5 -> 0, of which waited for: 5 -> 0; matrix products, arithmetic and copies ran while one was open for 3% -> 0% of each run, Pallas kernels for 0% -> 0%
where the time goes in v1:
time: 160 us; the launch traced here: 157 us
  Pallas kernels  155 us (97%)
    pallas_call x1, Pallas kernels, body(): pl.pallas_call(functools.partial(scatter_kernel, scale), out_shape=[jax.S...  147 us
    pallas_call x1, Pallas kernels, body(): pl.pallas_call(last_kernel, grid=(PER // 4,), in_specs=[pl.BlockSpec((NB,...  7.58 us

profile of v1, /device:TPU:34, one launch (start us, length us, event | category | flops | bytes accessed | tf_op | source)
XLA Modules:
  0.0 156.6 jit_solution(2581338930903130502)
XLA Ops:
  0.6 147.0 %scatter.1 = (f32[256,256]{1,0:T(8,128)}, f32[256,256]{1,0:T(8,128)}, bf16[32,256,256]{2,1,0:T(8,128)(2,1)}) custom-call(s32[16]{0:T(128)} %shifts.1, f32[16]{0:T(128)} %omega.1, bf16[32,256,256]{2,1,0:T(8,128)(2,1)} %bitcast.10, bf16[256,256]{1,0:T(8,128)(2,1)} %bitcast.12, bf16[256,128]{1,0:T(8,128)(2,1)} %bitcast.17, bf16[256,128]{1,0:T(8,128)(2,1)} %bitcast.18, ...), custom_call_target="tpu_custom_call" | custom-call | tf_op jit(solution)/shard_map/scatter/pallas_call | solution.py:393
  147.6 0.0 copy-start.1
  147.6 0.0 copy-start
  147.6 7.6 %last.1 = bf16[32,256,256]{2,1,0:T(8,128)(2,1)} custom-call(bf16[256,256]{1,0:T(8,128)(2,1)} %bitcast.13, bf16[32,256,256]{2,1,0:T(8,128)(2,1)} %get-tuple-element.8.turned), custom_call_target="tpu_custom_call" | custom-call | tf_op jit(solution)/shard_map/last/pallas_call | solution.py:428
  155.2 0.0 copy-done.1
  155.2 0.7 copy.13
  155.9 0.0 copy-done
  155.9 0.7 copy.14
Async XLA Ops:
  147.6 7.6 %copy-start.1 = (f32[256,256]{1,0:T(8,128)S(1)}, f32[256,256]{1,0:T(8,128)}, u32[]{:S(2)}) copy-start(f32[256,256]{1,0:T(8,128)} %get-tuple-element.6) | copy-start | bytes 786436
  147.6 8.3 %copy-start = (f32[256,256]{1,0:T(8,128)S(1)}, f32[256,256]{1,0:T(8,128)}, u32[]{:S(2)}) copy-start(f32[256,256]{1,0:T(8,128)} %get-tuple-element.7) | copy-start | bytes 786436

commit v2 on v1

--- a/solution.py
+++ b/solution.py
@@ -17,11 +17,13 @@
 PER = 32
 NB = 256
 HALF = 128
-CH = 4
+CH = 2
 STEPS = PER // CH
-AHEAD = 2
+AHEAD = 4
+LAG = 4
 W = 16
 CHIPS = 8
+LAST = 16
 ROWS = 32
 
 
@@ -42,8 +44,8 @@
 def scatter_kernel(
     scale, shifts, omega, green, grad, left_cpl, right_cpl, stiff,
     self_out, green_out, turned_out,
-    gpad, win, left_in, right_in, first, acc, part, sums, from_core, from_chip, rounded, mix, tile, turned,
-    g_sem, ls, lr, rs, rr, us, ur, c1s, c1r, c2s, c2r, gs, gr, fs, fr, ts,
+    gpad, win, left_in, right_in, first, acc, part, sums, from_core, from_chip, rounded, mix, tile, turned, held_over,
+    g_sem, ls, lr, rs, rr, us, ur, c1s, c1r, c2s, c2r, gs, gr, fs, fr, ts, hs, hr,
 ):
     me = lax.axis_index("energy")
     layer = lax.axis_index("layer")
@@ -74,6 +76,26 @@
             src_ref=win.at[pl.ds(PER + c * CH, CH)], dst_ref=win.at[pl.ds(c * CH, CH)],
             send_sem=us.at[c], recv_sem=ur.at[c],
             device_id={"energy": lax.rem(me + 1, 16), "layer": layer}, device_id_type=MESH)
+
+    crossing = 7
+
+    def relay_of(c):
+        return lax.rem(4 * lax.rem(c, 4), 6)
+
+    def relayed(c):
+        return lax.rem(c, 4) < 3
+
+    def aside_copy(c):
+        return pltpu.make_async_remote_copy(
+            src_ref=win.at[pl.ds(PER + c * CH, CH)], dst_ref=held_over.at[pl.ds(c // 4 * CH, CH)],
+            send_sem=us.at[c], recv_sem=hr.at[c // 4],
+            device_id={"energy": relay_of(c), "layer": layer}, device_id_type=MESH)
+
+    def relay_copy(c):
+        return pltpu.make_async_remote_copy(
+            src_ref=held_over.at[pl.ds(c // 4 * CH, CH)], dst_ref=win.at[pl.ds(c * CH, CH)],
+            send_sem=hs.at[c // 4], recv_sem=ur.at[c],
+            device_id={"energy": crossing + 1, "layer": layer}, device_id_type=MESH)
 
     def start_surfaces(c):
         @pl.when(has_right)
@@ -181,10 +203,16 @@
             total = nt(first[pl.ds(i * NB, NB), :], a) + nt(lp[i], lc) + nt(rp[i], rc)
             win[PER + e0 + i] = total.astype(BF)
 
-        @pl.when(has_upper)
+        aside = jnp.logical_and(me == crossing, relayed(c))
+
+        @pl.when(jnp.logical_and(has_upper, jnp.logical_not(aside)))
         def _():
             up_copy(c).start()
 
+        @pl.when(aside)
+        def _():
+            aside_copy(c).start()
+
         @pl.when(has_right)
         def _():
             left_copy(c).wait_send()
@@ -199,13 +227,20 @@
 
         correlate(PER + e0, PER + e0)
 
-        @pl.when(c > 0)
+        @pl.when(c >= LAG)
         def _():
             @pl.when(has_lower)
             def _():
-                up_copy(c - 1).wait_recv()
-
-            correlate(e0 - CH, e0 - CH)
+                up_copy(c - LAG).wait_recv()
+
+            correlate(e0 - LAG * CH, e0 - LAG * CH)
+
+        before = jnp.maximum(c - 1, 0)
+
+        @pl.when(jnp.logical_and(c > 0, jnp.logical_and(relayed(before), me == relay_of(before))))
+        def _():
+            aside_copy(before).wait_recv()
+            relay_copy(before).start()
 
         return carry
 
@@ -217,10 +252,13 @@
             device_id=partner, device_id_type=MESH)
 
     last = PER - CH
-
-    @pl.when(has_lower)
-    def _():
-        up_copy(STEPS - 1).wait_recv()
+    for c in range(STEPS - LAG, STEPS):
+        @pl.when(has_lower)
+        def _():
+            up_copy(c).wait_recv()
+
+        if c < STEPS - 1:
+            correlate(c * CH, c * CH)
 
     def finish(w, store):
         at = last + shifts[w]
@@ -370,6 +408,11 @@
         @pl.when(has_upper)
         def _():
             up_copy(c).wait_send()
+
+        if c % 4 < 3:
+            @pl.when(me == relay_of(c))
+            def _():
+                relay_copy(c).wait_send()
     for j in range(CHIPS):
         core_copy(j).wait_send()
         pass_on(j, core).wait_send()
@@ -378,10 +421,12 @@
         gather_copy(k).wait_send()
 
 
-def last_kernel(grad, turned, out):
+def last_kernel(grad, turned, self_in, green_in, out, self_out, green_out):
     a = grad[...]
-    for i in range(out.shape[0]):
+    for i in range(LAST):
         out[i] = nn(a, turned[i]).astype(BF)
+    self_out[...] = self_in[...]
+    green_out[...] = green_in[...]
 
 
 def body(green, gradient, left_coupling, right_coupling, dynamical, omega_sq, shifts):
@@ -414,25 +459,33 @@
             pltpu.VMEM((PER, NB, NB), F32),
             pltpu.VMEM((PER * ROWS, NB), BF),
             pltpu.VMEM((PER, NB, NB), BF),
+            pltpu.VMEM((PER // 4, NB, NB), BF),
             dma((STEPS,)),
             dma((STEPS,)), dma((STEPS,)), dma((STEPS,)), dma((STEPS,)), dma((STEPS,)), dma((STEPS,)),
             dma((CHIPS,)), dma((CHIPS,)), dma((CHIPS - 1,)), dma((CHIPS - 1,)),
             dma((CHIPS - 1,)), dma((CHIPS - 1,)), dma((CHIPS,)), dma((CHIPS,)),
-            dma((NB // ROWS,)),
+            dma((NB // ROWS,)), dma((STEPS // 4,)), dma((STEPS // 4,)),
         ],
         compiler_params=pltpu.CompilerParams(
             collective_id=0, has_side_effects=True, vmem_limit_bytes=58 << 20),
         name="scatter",
     )(shifts, omega_sq, green[:, 0], gradient[0], left_coupling[0], right_coupling[0], dynamical[0])
-    block = pl.BlockSpec((4, NB, NB), lambda i: (i, 0, 0))
-    electron = pl.pallas_call(
+    steps = PER // LAST
+    block = pl.BlockSpec((LAST, NB, NB), lambda i: (i, 0, 0))
+    whole = pl.BlockSpec((NB, NB), lambda i: (0, 0))
+    piece = pl.BlockSpec((NB // steps, NB), lambda i: (i, 0))
+    electron, own_self, own_green = pl.pallas_call(
         last_kernel,
-        grid=(PER // 4,),
-        in_specs=[pl.BlockSpec((NB, NB), lambda i: (0, 0)), block],
-        out_specs=block,
-        out_shape=jax.ShapeDtypeStruct((PER, NB, NB), BF),
+        grid=(steps,),
+        in_specs=[whole, block, piece, piece],
+        out_specs=[block, piece, piece],
+        out_shape=[
+            jax.ShapeDtypeStruct((PER, NB, NB), BF),
+            jax.ShapeDtypeStruct((NB, NB), F32),
+            jax.ShapeDtypeStruct((NB, NB), F32),
+        ],
         name="last",
-    )(gradient[0], turned)
+    )(gradient[0], turned, own_self, own_green)
     return own_self[None, None], own_green[None, None], electron[:, None]
 
 

time: 160 us -> 124 us (0.78); the launches traced: 157 us -> 124 us
  Pallas kernels: 155 us -> 123 us
    pallas_call x1, Pallas kernels: 147 us -> 119 us  [body(): pl.pallas_call(functools.partial(scatter_kernel, scale), out_shape=[jax.S...]
    pallas_call x1, Pallas kernels: 7.58 us -> 4.54 us  [body(): pl.pallas_call(last_kernel, grid=(steps,), in_specs=[whole, block, piece,...]
where the time goes in v2:
time: 124 us
  Pallas kernels  123 us (99%)
    pallas_call x1, Pallas kernels, body(): pl.pallas_call(functools.partial(scatter_kernel, scale), out_shape=[jax.S...  119 us
    pallas_call x1, Pallas kernels, body(): pl.pallas_call(last_kernel, grid=(steps,), in_specs=[whole, block, piece,...  4.54 us

profile of v2, /device:TPU:34, one launch (start us, length us, event | category | flops | bytes accessed | tf_op | source)
XLA Modules:
  0.0 123.7 jit_solution(1571423745993651628)
XLA Ops:
  0.6 118.5 %scatter.1 = (f32[256,256]{1,0:T(8,128)}, f32[256,256]{1,0:T(8,128)}, bf16[32,256,256]{2,1,0:T(8,128)(2,1)}) custom-call(s32[16]{0:T(128)} %shifts.1, f32[16]{0:T(128)} %omega.1, bf16[32,256,256]{2,1,0:T(8,128)(2,1)} %bitcast.10, bf16[256,256]{1,0:T(8,128)(2,1)} %bitcast.11, bf16[256,128]{1,0:T(8,128)(2,1)} %bitcast.14, bf16[256,128]{1,0:T(8,128)(2,1)} %bitcast.15, ...), custom_call_target="tpu_custom_call" | custom-call | tf_op jit(solution)/shard_map/scatter/pallas_call | solution.py:438
  119.2 4.5 %last.1 = (bf16[32,256,256]{2,1,0:T(8,128)(2,1)}, f32[256,256]{1,0:T(8,128)}, f32[256,256]{1,0:T(8,128)}) custom-call(bf16[256,256]{1,0:T(8,128)(2,1)} %bitcast.12, bf16[32,256,256]{2,1,0:T(8,128)(2,1)} %get-tuple-element.9.turned, f32[256,256]{1,0:T(8,128)} %get-tuple-element.10.self_in, f32[256,256]{1,0:T(8,128)} %get-tuple-element.11.green_in), custom_call_target="tpu_custom_call" | custom-call | tf_op jit(solution)/shard_map/last/pallas_call | solution.py:477

commit v3 on v2

--- a/solution.py
+++ b/solution.py
@@ -24,6 +24,9 @@
 W = 16
 CHIPS = 8
 LAST = 16
+SPLIT = 16
+QUAD = 4
+DOWN = SPLIT // 4
 ROWS = 32
 
 
@@ -44,8 +47,9 @@
 def scatter_kernel(
     scale, shifts, omega, green, grad, left_cpl, right_cpl, stiff,
     self_out, green_out, turned_out,
-    gpad, win, left_in, right_in, first, acc, part, sums, from_core, from_chip, rounded, mix, tile, turned, held_over,
+    gown, glow, win, left_in, right_in, first, acc, part, sums, from_core, from_chip, rounded, mix, tile, turned, held_over, held_green,
     g_sem, ls, lr, rs, rr, us, ur, c1s, c1r, c2s, c2r, gs, gr, fs, fr, ts, hs, hr,
+    low_sem, ds, dr, ks, kr,
 ):
     me = lax.axis_index("energy")
     layer = lax.axis_index("layer")
@@ -57,7 +61,7 @@
 
     def g_copy(c):
         return pltpu.make_async_copy(
-            green.at[pl.ds(c * CH, CH)], gpad.at[pl.ds(PER + c * CH, CH)], g_sem.at[c])
+            green.at[pl.ds(c * CH, CH)], gown.at[pl.ds(c * CH, CH)], g_sem.at[c])
 
     def left_copy(c):
         return pltpu.make_async_remote_copy(
@@ -97,7 +101,26 @@
             send_sem=hs.at[c // 4], recv_sem=ur.at[c],
             device_id={"energy": crossing + 1, "layer": layer}, device_id_type=MESH)
 
-    def start_surfaces(c):
+    def down_copy(p):
+        return pltpu.make_async_remote_copy(
+            src_ref=green.at[pl.ds(p * DOWN, DOWN)], dst_ref=gown.at[pl.ds(PER + p * DOWN, DOWN)],
+            send_sem=ds.at[p], recv_sem=dr.at[p],
+            device_id={"energy": lax.rem(me + 15, 16), "layer": layer}, device_id_type=MESH)
+
+    def down_aside(p):
+        return pltpu.make_async_remote_copy(
+            src_ref=green.at[pl.ds(p * DOWN, DOWN)], dst_ref=held_green, send_sem=ds.at[p], recv_sem=kr,
+            device_id={"energy": 14 - 2 * p, "layer": layer}, device_id_type=MESH)
+
+    def down_relay(p):
+        return pltpu.make_async_remote_copy(
+            src_ref=held_green, dst_ref=gown.at[pl.ds(PER + p * DOWN, DOWN)], send_sem=ks, recv_sem=dr.at[p],
+            device_id={"energy": crossing, "layer": layer}, device_id_type=MESH)
+
+    low_copy = pltpu.make_async_copy(green.at[pl.ds(SPLIT, PER - SPLIT)], glow.at[pl.ds(PER, PER - SPLIT)], low_sem)
+
+    def start_surfaces(step):
+        c = STEPS - 1 - step
         @pl.when(has_right)
         def _():
             left_copy(c).start()
@@ -106,8 +129,9 @@
         def _():
             right_copy(c).start()
 
-    for c in range(STEPS):
+    for c in reversed(range(STEPS)):
         g_copy(c).start()
+    low_copy.start()
 
     barrier = pltpu.get_barrier_semaphore()
     for k in range(1, 16):
@@ -127,13 +151,33 @@
     for c in range(AHEAD):
         start_surfaces(c)
 
+    for p in range(4):
+        split_path = me == crossing + 1 if p < 3 else me < 0
+
+        @pl.when(jnp.logical_and(has_lower, jnp.logical_not(split_path)))
+        def _():
+            down_copy(p).start()
+
+        @pl.when(split_path)
+        def _():
+            down_aside(p).start()
+
     def clear(i, carry):
         zero = jnp.zeros((NB, NB), BF)
-        gpad[i] = zero
-        gpad[2 * PER + i] = zero
+        glow[i] = zero
         return carry
 
     lax.fori_loop(0, PER, clear, 0)
+
+    def clear_top(i, carry):
+        gown[i] = jnp.zeros((NB, NB), BF)
+        return carry
+
+    lax.fori_loop(PER + SPLIT, 2 * PER, clear_top, 0)
+
+    @pl.when(jnp.logical_not(has_upper))
+    def _():
+        lax.fori_loop(PER, PER + SPLIT, clear_top, 0)
 
     @pl.when(jnp.logical_not(has_lower))
     def _():
@@ -167,14 +211,15 @@
 
     for c in range(STEPS):
         g_copy(c).wait()
-
-    def correlate(s_base, g_base):
+    low_copy.wait()
+
+    def correlate(s_base, green_ref, g_base):
         def one(t, carry):
             rows = pl.ds(pl.multiple_of(t * ROWS, ROWS), ROWS)
-            held = [win[s_base + i, rows, :] for i in range(CH)]
+            held = [win[s_base + i, rows, :] for i in range(QUAD)]
             for w in range(W):
                 at = g_base + shifts[w]
-                terms = [held[i] * gpad[at + i, rows, :] for i in range(CH)]
+                terms = [held[i] * green_ref[at + i, rows, :] for i in range(QUAD)]
                 acc[w, rows, :] += tree(terms).astype(F32)
             return carry
 
@@ -184,10 +229,11 @@
     lc = left_cpl[...]
     rc = right_cpl[...]
 
-    def step(c, carry):
+    def step(at_step, carry):
+        c = STEPS - 1 - at_step
         e0 = c * CH
         for i in range(CH):
-            first[pl.ds(i * NB, NB), :] = nn(a, gpad[PER + e0 + i]).astype(BF)
+            first[pl.ds(i * NB, NB), :] = nn(a, gown[e0 + i]).astype(BF)
 
         @pl.when(has_left)
         def _():
@@ -203,9 +249,11 @@
             total = nt(first[pl.ds(i * NB, NB), :], a) + nt(lp[i], lc) + nt(rp[i], rc)
             win[PER + e0 + i] = total.astype(BF)
 
-        aside = jnp.logical_and(me == crossing, relayed(c))
-
-        @pl.when(jnp.logical_and(has_upper, jnp.logical_not(aside)))
+        needed = c >= SPLIT // CH
+        aside = jnp.logical_and(me == crossing, jnp.logical_and(needed, relayed(c)))
+        later = jnp.logical_and(me == crossing, jnp.logical_not(needed))
+
+        @pl.when(jnp.logical_and(has_upper, jnp.logical_not(jnp.logical_or(aside, later))))
         def _():
             up_copy(c).start()
 
@@ -221,51 +269,68 @@
         def _():
             right_copy(c).wait_send()
 
-        @pl.when(c + AHEAD < STEPS)
-        def _():
-            start_surfaces(c + AHEAD)
-
-        correlate(PER + e0, PER + e0)
-
-        @pl.when(c >= LAG)
+        @pl.when(at_step + AHEAD < STEPS)
+        def _():
+            start_surfaces(at_step + AHEAD)
+
+        low = c + LAG
+        pair = jnp.logical_and(low < STEPS, jnp.logical_and(low >= SPLIT // CH, lax.rem(at_step - LAG + 2 * STEPS, 2) == 1))
+
+        @pl.when(pair)
         def _():
             @pl.when(has_lower)
             def _():
-                up_copy(c - LAG).wait_recv()
-
-            correlate(e0 - LAG * CH, e0 - LAG * CH)
-
-        before = jnp.maximum(c - 1, 0)
-
-        @pl.when(jnp.logical_and(c > 0, jnp.logical_and(relayed(before), me == relay_of(before))))
+                up_copy(low + 1).wait_recv()
+                up_copy(low).wait_recv()
+
+            correlate(low * CH, glow, low * CH - SPLIT)
+
+        @pl.when(at_step == STEPS // 2)
+        def _():
+            @pl.when(has_upper)
+            def _():
+                for p in range(4):
+                    down_copy(p).wait_recv()
+
+        @pl.when(jnp.logical_and(at_step >= STEPS // 2, c > 0))
+        def _():
+            top = PER - QUAD - (at_step - STEPS // 2) * QUAD
+            correlate(PER + top, gown, top)
+
+        before = jnp.minimum(c + 1, STEPS - 1)
+
+        @pl.when(jnp.logical_and(
+            jnp.logical_and(at_step > 0, before >= SPLIT // CH), jnp.logical_and(relayed(before), me == relay_of(before))))
         def _():
             aside_copy(before).wait_recv()
             relay_copy(before).start()
 
+        for p in range(3):
+            @pl.when(jnp.logical_and(at_step == 2, me == 14 - 2 * p))
+            def _():
+                down_aside(p).wait_recv()
+                down_relay(p).start()
+
         return carry
 
     lax.fori_loop(0, STEPS, step, 0)
+
+    for c in reversed(range(SPLIT // CH)):
+        @pl.when(me == crossing)
+        def _():
+            (aside_copy(c) if c % 4 < 3 else up_copy(c)).start()
 
     def core_copy(j):
         return pltpu.make_async_remote_copy(
             src_ref=part.at[j], dst_ref=from_core.at[j], send_sem=c1s.at[j], recv_sem=c1r.at[j],
             device_id=partner, device_id_type=MESH)
 
-    last = PER - CH
-    for c in range(STEPS - LAG, STEPS):
-        @pl.when(has_lower)
-        def _():
-            up_copy(c).wait_recv()
-
-        if c < STEPS - 1:
-            correlate(c * CH, c * CH)
-
     def finish(w, store):
-        at = last + shifts[w]
+        at = shifts[w]
 
         def one(t, carry):
             rows = pl.ds(pl.multiple_of(t * ROWS, ROWS), ROWS)
-            terms = [win[last + i, rows, :] * gpad[at + i, rows, :] for i in range(CH)]
+            terms = [win[PER + i, rows, :] * gown[at + i, rows, :] for i in range(QUAD)]
             store(rows, (acc[w, rows, :] + tree(terms).astype(F32)) * scale)
             return carry
 
@@ -315,6 +380,14 @@
         return carry
 
     lax.fori_loop(1, CHIPS, join, 0)
+
+    for c in reversed(range(SPLIT // CH)):
+        if c % 4 < 3:
+            @pl.when(me == relay_of(c))
+            def _():
+                aside_copy(c).wait_recv()
+                relay_copy(c).start()
+
     core_copy(chip).wait_recv()
     for k in range(1, CHIPS):
         chip_copy(k).wait_recv()
@@ -362,6 +435,11 @@
     pass_on(0, core).start()
     for k in range(1, CHIPS):
         gather_copy(k).start()
+
+    for c in range(SPLIT // CH):
+        @pl.when(has_lower)
+        def _():
+            up_copy(c).wait_recv()
 
     group = 4
     for g in range(W // group):
@@ -413,6 +491,15 @@
             @pl.when(me == relay_of(c))
             def _():
                 relay_copy(c).wait_send()
+    for p in range(4):
+        @pl.when(has_lower)
+        def _():
+            down_copy(p).wait_send()
+
+        if p < 3:
+            @pl.when(me == 14 - 2 * p)
+            def _():
+                down_relay(p).wait_send()
     for j in range(CHIPS):
         core_copy(j).wait_send()
         pass_on(j, core).wait_send()
@@ -445,7 +532,8 @@
         in_specs=[smem, smem, hbm, vmem, vmem, vmem, vmem],
         out_specs=[vmem, vmem, hbm],
         scratch_shapes=[
-            pltpu.VMEM((3 * PER, NB, NB), BF),
+            pltpu.VMEM((2 * PER, NB, NB), BF),
+            pltpu.VMEM((2 * PER - SPLIT, NB, NB), BF),
             pltpu.VMEM((2 * PER, NB, NB), BF),
             pltpu.VMEM((PER, HALF, HALF), BF),
             pltpu.VMEM((PER, HALF, HALF), BF),
@@ -460,11 +548,13 @@
             pltpu.VMEM((PER * ROWS, NB), BF),
             pltpu.VMEM((PER, NB, NB), BF),
             pltpu.VMEM((PER // 4, NB, NB), BF),
+            pltpu.VMEM((DOWN, NB, NB), BF),
             dma((STEPS,)),
             dma((STEPS,)), dma((STEPS,)), dma((STEPS,)), dma((STEPS,)), dma((STEPS,)), dma((STEPS,)),
             dma((CHIPS,)), dma((CHIPS,)), dma((CHIPS - 1,)), dma((CHIPS - 1,)),
             dma((CHIPS - 1,)), dma((CHIPS - 1,)), dma((CHIPS,)), dma((CHIPS,)),
             dma((NB // ROWS,)), dma((STEPS // 4,)), dma((STEPS // 4,)),
+            dma, dma((4,)), dma((4,)), dma, dma,
         ],
         compiler_params=pltpu.CompilerParams(
             collective_id=0, has_side_effects=True, vmem_limit_bytes=58 << 20),

time: 124 us -> 117 us (0.944)
  the two profiles are of different devices: /device:TPU:34 before, /device:TPU:49 now
where the time goes in v3:
time: 117 us
  Pallas kernels  116 us (99%)
    pallas_call x1, Pallas kernels, body(): pl.pallas_call(functools.partial(scatter_kernel, scale), out_shape=[jax.S...  112 us
    pallas_call x1, Pallas kernels, body(): pl.pallas_call(last_kernel, grid=(steps,), in_specs=[whole, block, piece,...  4.54 us

profile of v3, /device:TPU:49, one launch (start us, length us, event | category | flops | bytes accessed | tf_op | source)
XLA Modules:
  0.0 116.9 jit_solution(9512966570064966285)
XLA Ops:
  0.6 111.8 %scatter.1 = (f32[256,256]{1,0:T(8,128)}, f32[256,256]{1,0:T(8,128)}, bf16[32,256,256]{2,1,0:T(8,128)(2,1)}) custom-call(s32[16]{0:T(128)} %shifts.1, f32[16]{0:T(128)} %omega.1, bf16[32,256,256]{2,1,0:T(8,128)(2,1)} %bitcast.10, bf16[256,256]{1,0:T(8,128)(2,1)} %bitcast.11, bf16[256,128]{1,0:T(8,128)(2,1)} %bitcast.14, bf16[256,128]{1,0:T(8,128)(2,1)} %bitcast.15, ...), custom_call_target="tpu_custom_call" | custom-call | tf_op jit(solution)/shard_map/scatter/pallas_call | solution.py:525
  112.4 4.5 %last.1 = (bf16[32,256,256]{2,1,0:T(8,128)(2,1)}, f32[256,256]{1,0:T(8,128)}, f32[256,256]{1,0:T(8,128)}) custom-call(bf16[256,256]{1,0:T(8,128)(2,1)} %bitcast.12, bf16[32,256,256]{2,1,0:T(8,128)(2,1)} %get-tuple-element.9.turned, f32[256,256]{1,0:T(8,128)} %get-tuple-element.10.self_in, f32[256,256]{1,0:T(8,128)} %get-tuple-element.11.green_in), custom_call_target="tpu_custom_call" | custom-call | tf_op jit(solution)/shard_map/last/pallas_call | solution.py:567

commit v4 on v3

--- a/solution.py
+++ b/solution.py
@@ -23,6 +23,8 @@
 LAG = 4
 W = 16
 CHIPS = 8
+PLACES = ((0, 0), (1, 0), (0, 1), (0, 3), (1, 1), (1, 3), (0, 2), (1, 2))
+STAGES = [[1, 2, 3], [4, 5, 6, 7]]
 LAST = 16
 SPLIT = 16
 QUAD = 4
@@ -38,6 +40,15 @@
     return lax.dot_general(a, b, (((1,), (1,)), ((), ())), preferred_element_type=F32, **kw)
 
 
+def halves(a):
+    high = a.astype(BF)
+    return high, (a - high.astype(F32)).astype(BF)
+
+
+def nn_split(a, b):
+    return nn(a[0], b[0]) + (nn(a[0], b[1]) + nn(a[1], b[0]))
+
+
 def tree(terms):
     while len(terms) > 1:
         terms = [terms[i] + terms[i + 1] if i + 1 < len(terms) else terms[i] for i in range(0, len(terms), 2)]
@@ -46,8 +57,8 @@
 
 def scatter_kernel(
     scale, shifts, omega, green, grad, left_cpl, right_cpl, stiff,
-    self_out, green_out, turned_out,
-    gown, glow, win, left_in, right_in, first, acc, part, sums, from_core, from_chip, rounded, mix, tile, turned, held_over, held_green,
+    self_out, green_out, mixture_out,
+    gown, glow, win, left_in, right_in, first, acc, part, sums, from_core, from_chip, rounded, mix, mixture, held_over, held_green,
     g_sem, ls, lr, rs, rr, us, ur, c1s, c1r, c2s, c2r, gs, gr, fs, fr, ts, hs, hr,
     low_sem, ds, dr, ks, kr,
 ):
@@ -409,76 +420,91 @@
     inv_row = 1.0 / jnp.sum(diag, axis=0, keepdims=True)
     inv_col = 1.0 / jnp.sum(diag, axis=1, keepdims=True)
     approx = jnp.where(on_diag, 2.0 * inv_col, 0.0) - inv_col * (matrix * inv_row)
+    matrix_halves = halves(matrix)
     for _ in range(NEWTON - 1):
-        product = nn(matrix, approx, precision=lax.Precision.HIGHEST)
-        approx = 2.0 * approx - nn(approx, product, precision=lax.Precision.HIGHEST)
+        approx_halves = halves(approx)
+        product = nn_split(matrix_halves, approx_halves)
+        approx = 2.0 * approx - nn_split(approx_halves, halves(product))
     green_out[...] = approx
     rounded[me] = approx.astype(BF)
 
+    row, column = lax.rem(chip, 4), chip // 4
+
+    def chip_at(k):
+        dx, dy = PLACES[k]
+        return lax.rem(column + dx, 2) * 4 + lax.rem(row + dy, 4)
+
+    def chip_from(k):
+        dx, dy = PLACES[k]
+        return lax.rem(column + dx, 2) * 4 + lax.rem(row + 4 - dy, 4)
+
     def gather_copy(k):
         return pltpu.make_async_remote_copy(
             src_ref=rounded.at[me], dst_ref=rounded.at[me], send_sem=gs.at[k - 1], recv_sem=gr.at[k - 1],
-            device_id={"energy": 2 * lax.rem(chip + k, CHIPS) + core, "layer": layer}, device_id_type=MESH)
+            device_id={"energy": 2 * chip_at(k) + core, "layer": layer}, device_id_type=MESH)
 
     def gather_arrival(k):
-        w = 2 * lax.rem(chip + CHIPS - k, CHIPS) + core
+        w = 2 * chip_from(k) + core
         return pltpu.make_async_remote_copy(
             src_ref=rounded.at[w], dst_ref=rounded.at[w], send_sem=gs.at[k - 1], recv_sem=gr.at[k - 1],
             device_id={"energy": w, "layer": layer}, device_id_type=MESH)
 
     def pass_on(k, whose):
-        w = 2 * lax.rem(chip + CHIPS - k, CHIPS) + whose
+        w = 2 * chip_from(k) + whose
         return pltpu.make_async_remote_copy(
             src_ref=rounded.at[w], dst_ref=rounded.at[w], send_sem=fs.at[k], recv_sem=fr.at[k],
             device_id=partner, device_id_type=MESH)
 
-    pass_on(0, core).start()
-    for k in range(1, CHIPS):
-        gather_copy(k).start()
-
-    for c in range(SPLIT // CH):
-        @pl.when(has_lower)
-        def _():
-            up_copy(c).wait_recv()
-
-    group = 4
-    for g in range(W // group):
+    def turn_copy(t):
+        rows = pl.ds(pl.multiple_of(t * ROWS, ROWS), ROWS)
+        return pltpu.make_async_copy(mixture.at[:, rows, :], mixture_out.at[:, rows, :], ts.at[t])
+
+    def add_group(pair, start, final):
         ws = []
-        for k in (2 * g, 2 * g + 1):
-            if k > 0:
-                gather_arrival(k).wait_recv()
-                pass_on(k, core).start()
-        for k in (2 * g, 2 * g + 1):
+        for k in pair:
             pass_on(k, 1 - core).wait_recv()
-            owner = 2 * lax.rem(chip + CHIPS - k, CHIPS)
-            ws += [owner, owner + 1]
-        final = g == W // group - 1
+            ws += [2 * chip_from(k), 2 * chip_from(k) + 1]
 
         def mix_rows(t, carry):
             rows = pl.ds(pl.multiple_of(t * ROWS, ROWS), ROWS)
             held = [rounded[w, rows, :] for w in ws]
             ats = [PER - shifts[w] for w in ws]
             for e in range(PER):
-                terms = [held[i] * win[ats[i] + e, rows, :] for i in range(group)]
-                value = tree(terms).astype(F32)
-                if g > 0:
+                value = tree([held[i] * win[ats[i] + e, rows, :] for i in range(len(ws))]).astype(F32)
+                if not start:
                     value = mix[e, rows, :] + value
                 if final:
-                    tile[pl.ds(e * ROWS, ROWS), :] = value.astype(BF)
+                    mixture[e, rows, :] = value.astype(BF)
                 else:
                     mix[e, rows, :] = value
             if final:
-                out = nt(tile[...], a).astype(BF)
-                for e in range(PER):
-                    turned[e, rows, :] = out[e * ROWS:(e + 1) * ROWS]
                 turn_copy(t).start()
             return carry
 
-        def turn_copy(t):
-            rows = pl.ds(pl.multiple_of(t * ROWS, ROWS), ROWS)
-            return pltpu.make_async_copy(turned.at[:, rows, :], turned_out.at[:, rows, :], ts.at[t])
-
         lax.fori_loop(0, NB // ROWS, mix_rows, 0)
+
+    pass_on(0, core).start()
+    groups = [(0, 1), (2, 3), (4, 5), (6, 7)]
+    for k in STAGES[0]:
+        gather_copy(k).start()
+    for c in range(SPLIT // CH):
+        @pl.when(has_lower)
+        def _():
+            up_copy(c).wait_recv()
+
+    ready = [0]
+    for i, stage in enumerate(STAGES):
+        for k in stage:
+            gather_copy(k).wait_send()
+        for k in STAGES[i + 1] if i + 1 < len(STAGES) else ():
+            gather_copy(k).start()
+        for k in stage:
+            gather_arrival(k).wait_recv()
+            pass_on(k, core).start()
+        ready += stage
+        while groups and all(k in ready for k in groups[0]):
+            pair = groups.pop(0)
+            add_group(pair, 0 in pair, not groups)
 
     for t in range(NB // ROWS):
         turn_copy(t).wait()
@@ -505,13 +531,13 @@
         pass_on(j, core).wait_send()
     for k in range(1, CHIPS):
         chip_copy(k).wait_send()
-        gather_copy(k).wait_send()
-
-
-def last_kernel(grad, turned, self_in, green_in, out, self_out, green_out):
+
+
+def last_kernel(grad, mixture, self_in, green_in, out, self_out, green_out, second):
     a = grad[...]
     for i in range(LAST):
-        out[i] = nn(a, turned[i]).astype(BF)
+        second[pl.ds(i * NB, NB), :] = nn(a, mixture[i]).astype(BF)
+    out[...] = nt(second[...], a).astype(BF).reshape(LAST, NB, NB)
     self_out[...] = self_in[...]
     green_out[...] = green_in[...]
 
@@ -522,7 +548,7 @@
     smem = pl.BlockSpec(memory_space=pltpu.SMEM)
     hbm = pl.BlockSpec(memory_space=pl.ANY)
     dma = pltpu.SemaphoreType.DMA
-    own_self, own_green, turned = pl.pallas_call(
+    own_self, own_green, mixture = pl.pallas_call(
         functools.partial(scatter_kernel, scale),
         out_shape=[
             jax.ShapeDtypeStruct((NB, NB), F32),
@@ -545,7 +571,6 @@
             pltpu.VMEM((CHIPS - 1, NB, NB), BF),
             pltpu.VMEM((W, NB, NB), BF),
             pltpu.VMEM((PER, NB, NB), F32),
-            pltpu.VMEM((PER * ROWS, NB), BF),
             pltpu.VMEM((PER, NB, NB), BF),
             pltpu.VMEM((PER // 4, NB, NB), BF),
             pltpu.VMEM((DOWN, NB, NB), BF),
@@ -574,8 +599,10 @@
             jax.ShapeDtypeStruct((NB, NB), F32),
             jax.ShapeDtypeStruct((NB, NB), F32),
         ],
+        scratch_shapes=[pltpu.VMEM((LAST * NB, NB), BF)],
+        compiler_params=pltpu.CompilerParams(vmem_limit_bytes=60 << 20),
         name="last",
-    )(gradient[0], turned, own_self, own_green)
+    )(gradient[0], mixture, own_self, own_green)
     return own_self[None, None], own_green[None, None], electron[:, None]
 
 

time: 117 us -> 117 us (level)
  the two profiles are of different devices: /device:TPU:49 before, /device:TPU:34 now
where the time goes in v4:
time: 117 us; the launch traced here: 115 us
  Pallas kernels  114 us (97%)
    pallas_call x1, Pallas kernels, body(): pl.pallas_call(functools.partial(scatter_kernel, scale), out_shape=[jax.S...  109 us
    pallas_call x1, Pallas kernels, body(): pl.pallas_call(last_kernel, grid=(steps,), in_specs=[whole, block, piece,...  5.6 us

profile of v4, /device:TPU:34, one launch (start us, length us, event | category | flops | bytes accessed | tf_op | source)
XLA Modules:
  0.0 115.1 jit_solution(16719867712029605271)
XLA Ops:
  0.6 108.8 %scatter.1 = (f32[256,256]{1,0:T(8,128)}, f32[256,256]{1,0:T(8,128)}, bf16[32,256,256]{2,1,0:T(8,128)(2,1)}) custom-call(s32[16]{0:T(128)} %shifts.1, f32[16]{0:T(128)} %omega.1, bf16[32,256,256]{2,1,0:T(8,128)(2,1)} %bitcast.10, bf16[256,256]{1,0:T(8,128)(2,1)} %bitcast.11, bf16[256,128]{1,0:T(8,128)(2,1)} %bitcast.14, bf16[256,128]{1,0:T(8,128)(2,1)} %bitcast.15, ...), custom_call_target="tpu_custom_call" | custom-call | tf_op jit(solution)/shard_map/scatter/pallas_call | solution.py:551
  109.5 5.6 %last.1 = (bf16[32,256,256]{2,1,0:T(8,128)(2,1)}, f32[256,256]{1,0:T(8,128)}, f32[256,256]{1,0:T(8,128)}) custom-call(bf16[256,256]{1,0:T(8,128)(2,1)} %bitcast.12, bf16[32,256,256]{2,1,0:T(8,128)(2,1)} %get-tuple-element.9.mixture, f32[256,256]{1,0:T(8,128)} %get-tuple-element.10.self_in, f32[256,256]{1,0:T(8,128)} %get-tuple-element.11.green_in), custom_call_target="tpu_custom_call" | custom-call | tf_op jit(solution)/shard_map/last/pallas_call | solution.py:592

commit v5 on v4

--- a/solution.py
+++ b/solution.py
@@ -24,7 +24,7 @@
 W = 16
 CHIPS = 8
 PLACES = ((0, 0), (1, 0), (0, 1), (0, 3), (1, 1), (1, 3), (0, 2), (1, 2))
-STAGES = [[1, 2, 3], [4, 5, 6, 7]]
+STAGES = [[1, 2, 3, 4, 5], [6, 7]]
 LAST = 16
 SPLIT = 16
 QUAD = 4
@@ -487,11 +487,6 @@
     groups = [(0, 1), (2, 3), (4, 5), (6, 7)]
     for k in STAGES[0]:
         gather_copy(k).start()
-    for c in range(SPLIT // CH):
-        @pl.when(has_lower)
-        def _():
-            up_copy(c).wait_recv()
-
     ready = [0]
     for i, stage in enumerate(STAGES):
         for k in stage:
@@ -501,6 +496,11 @@
         for k in stage:
             gather_arrival(k).wait_recv()
             pass_on(k, core).start()
+        for c in range(SPLIT // CH if i == 0 else 0):
+            @pl.when(has_lower)
+            def _():
+                up_copy(c).wait_recv()
+
         ready += stage
         while groups and all(k in ready for k in groups[0]):
             pair = groups.pop(0)

time: 117 us -> 116 us (level)
  no operation moved by 1% of the time
where the time goes in v5:
time: 116 us; the launch traced here: 114 us
  Pallas kernels  114 us (98%)
    pallas_call x1, Pallas kernels, body(): pl.pallas_call(functools.partial(scatter_kernel, scale), out_shape=[jax.S...  108 us
    pallas_call x1, Pallas kernels, body(): pl.pallas_call(last_kernel, grid=(steps,), in_specs=[whole, block, piece,...  5.6 us

profile of v5, /device:TPU:34, one launch (start us, length us, event | category | flops | bytes accessed | tf_op | source)
XLA Modules:
  0.0 114.2 jit_solution(62843958138683481)
XLA Ops:
  0.6 107.9 %scatter.1 = (f32[256,256]{1,0:T(8,128)}, f32[256,256]{1,0:T(8,128)}, bf16[32,256,256]{2,1,0:T(8,128)(2,1)}) custom-call(s32[16]{0:T(128)} %shifts.1, f32[16]{0:T(128)} %omega.1, bf16[32,256,256]{2,1,0:T(8,128)(2,1)} %bitcast.10, bf16[256,256]{1,0:T(8,128)(2,1)} %bitcast.11, bf16[256,128]{1,0:T(8,128)(2,1)} %bitcast.14, bf16[256,128]{1,0:T(8,128)(2,1)} %bitcast.15, ...), custom_call_target="tpu_custom_call" | custom-call | tf_op jit(solution)/shard_map/scatter/pallas_call | solution.py:551
  108.6 5.6 %last.1 = (bf16[32,256,256]{2,1,0:T(8,128)(2,1)}, f32[256,256]{1,0:T(8,128)}, f32[256,256]{1,0:T(8,128)}) custom-call(bf16[256,256]{1,0:T(8,128)(2,1)} %bitcast.12, bf16[32,256,256]{2,1,0:T(8,128)(2,1)} %get-tuple-element.9.mixture, f32[256,256]{1,0:T(8,128)} %get-tuple-element.10.self_in, f32[256,256]{1,0:T(8,128)} %get-tuple-element.11.green_in), custom_call_target="tpu_custom_call" | custom-call | tf_op jit(solution)/shard_map/last/pallas_call | solution.py:592
